TPU v7x, 128 devices: a whole 4x4x4 slice. The times are simulated.
128 devices in a mesh: dp: 8 (over z, core), tensor: 16 (over y, x).
Axes of the slice: x: 4, y: 4, z: 4, core: 2. Of those that a mesh axis runs over, the one named last changes fastest.
Arguments:
- kept_block_input: bfloat16 [8, 128, 16384], P('dp', 'tensor'), may hold values from -6 to 6
- block_output_gradient: bfloat16 [8, 128, 16384], P('dp', 'tensor'), may hold values from -6 to 6
- gate_preact_kept: bfloat16 [8, 128, 26624], P('dp', None, 'tensor'), may hold values from -8 to 8
- up_preact_kept: bfloat16 [8, 128, 26624], P('dp', None, 'tensor'), may hold values from -6 to 6
- gate_weight: bfloat16 [16384, 26624], P('dp', 'tensor'), may hold values from -0.046875 to 0.046875
- up_weight: bfloat16 [16384, 26624], P('dp', 'tensor'), may hold values from -0.046875 to 0.046875
- down_weight: bfloat16 [26624, 16384], P('tensor', 'dp'), may hold values from -0.0390625 to 0.0390625
- adapter_down_maps: bfloat16 [2, 16, 16384], replicated, may hold values from -0.046875 to 0.046875
- adapter_up_maps: bfloat16 [2, 16, 26624], P(None, None, 'tensor'), may hold values from -0.0390625 to 0.0390625
Outputs:
- block_input_gradient: bfloat16 [8, 128, 16384], P('dp', 'tensor')
- adapter_down_gradient: float32 [2, 16, 16384], replicated
- adapter_up_gradient: float32 [2, 16, 26624], P(None, None, 'tensor')
All inputs are finite; a program needn't handle non-finite values.
Results may differ from a plain program's by a relative error of at most 0.019.
Values may be sent and summed in bfloat16 or wider, within the bound.
A program may use at most 128 MiB of HBM per device.

v0:
```python
import jax
import jax.numpy as jnp
from jax import lax
from jax.sharding import PartitionSpec as P

HB = 128


ADAPTER_SCALE = 2.0


def hadamard(length):
    positions = jnp.arange(length, dtype=jnp.int32)
    common_bits = jnp.bitwise_and(positions[:, None], positions[None, :])
    parity = jnp.zeros((length, length), jnp.int32)
    for bit_index in range(length.bit_length() - 1):
        parity = parity + jnp.bitwise_and(jnp.right_shift(common_bits, bit_index), 1)
    signs = (1 - 2 * (parity % 2)).astype(jnp.float32)
    return signs / jnp.sqrt(jnp.float32(length))


def rotate(values):
    table = hadamard(HB)
    array_shape = values.shape
    blocks = values.astype(jnp.float32).reshape((-1, array_shape[-1] // HB, HB))
    turned = jnp.einsum("tkb,bc->tkc", blocks, table, precision=lax.Precision.HIGHEST)
    return turned.reshape(array_shape).astype(jnp.bfloat16)


def swiglu_grads(hidden_grad, gate_in, up_in):
    gate_pre = gate_in.astype(jnp.float32)
    up_pre = up_in.astype(jnp.float32)
    squash = jax.nn.sigmoid(gate_pre)
    gate_gradient = (hidden_grad * up_pre * squash * (1.0 + gate_pre * (1.0 - squash))).astype(
        jnp.bfloat16
    )
    up_gradient = (hidden_grad * gate_pre * squash).astype(jnp.bfloat16)
    return (gate_gradient, up_gradient)


def contract_trailing(left, right):
    return lax.dot_general(
        left, right, (((2,), (1,)), ((), ())), preferred_element_type=jnp.float32
    )


def on_device(
    kept_block_input,
    block_output_gradient,
    gate_preact_kept,
    up_preact_kept,
    gate_weight,
    up_weight,
    down_weight,
    adapter_down_maps,
    adapter_up_maps,
):
    width_of_model = kept_block_input.shape[2]
    adapter_rank_count = adapter_down_maps.shape[1]
    group_index = lax.axis_index("dp")
    inputs = rotate(kept_block_input)
    grads = rotate(block_output_gradient)
    adapter_lookup = adapter_down_maps.reshape(2 * adapter_rank_count, width_of_model)
    adapter_own = jnp.dot(inputs[0], adapter_lookup.T, preferred_element_type=jnp.float32).astype(
        jnp.bfloat16
    )[None]
    grad_split = lax.all_to_all(grads, "dp", split_axis=2, concat_axis=0, tiled=True)
    grad_rows, adapter_rows = (
        lax.all_gather(grad_split, "tensor", axis=1, tiled=True),
        lax.all_gather(adapter_own, "tensor", axis=1, tiled=True),
    )
    slice_width = grad_rows.shape[2]
    group_token_count = grad_rows.shape[1]
    token_groups = grad_rows.shape[0]
    hidden_part = contract_trailing(grad_rows, down_weight)
    hidden_grad = lax.psum_scatter(hidden_part, "dp", scatter_dimension=0, tiled=True)
    dgate_own, dup_own = swiglu_grads(hidden_grad, gate_preact_kept, up_preact_kept)
    gate_gradient_full, up_gradient_full = (
        lax.all_gather(dgate_own, "dp", axis=0, tiled=True),
        lax.all_gather(dup_own, "dp", axis=0, tiled=True),
    )
    gradient_scale = ADAPTER_SCALE / (token_groups * group_token_count) ** 0.5
    token_dims = (((0, 1), (0, 1)), ((), ()))
    gate_up_map = lax.dot_general(
        adapter_rows[:, :, :adapter_rank_count],
        dgate_own,
        token_dims,
        preferred_element_type=jnp.float32,
    )
    up_branch_map = lax.dot_general(
        adapter_rows[:, :, adapter_rank_count:],
        dup_own,
        token_dims,
        preferred_element_type=jnp.float32,
    )
    adapter_up_gradient = (
        lax.psum(jnp.stack([gate_up_map, up_branch_map]).astype(jnp.bfloat16), "dp").astype(
            jnp.float32
        )
        * gradient_scale
    )
    gate_rank_value = contract_trailing(gate_gradient_full, adapter_up_maps[0])
    up_rank_value = contract_trailing(up_gradient_full, adapter_up_maps[1])
    rank_part = jnp.concatenate([gate_rank_value, up_rank_value], axis=2)
    adapter_cols = lax.dynamic_slice_in_dim(
        adapter_lookup, group_index * slice_width, slice_width, 1
    ).astype(jnp.float32)
    input_partial = contract_trailing(gate_gradient_full, gate_weight) + contract_trailing(
        up_gradient_full, up_weight
    )
    input_partial = input_partial + ADAPTER_SCALE * lax.dot_general(
        rank_part,
        adapter_cols,
        (((2,), (0,)), ((), ())),
        precision=lax.Precision.HIGHEST,
        preferred_element_type=jnp.float32,
    )
    input_sum, rank_sum = (
        lax.psum_scatter(
            input_partial.astype(jnp.bfloat16), "tensor", scatter_dimension=1, tiled=True
        ).astype(jnp.float32),
        lax.psum_scatter(
            rank_part.astype(jnp.bfloat16), "tensor", scatter_dimension=1, tiled=True
        ).astype(jnp.float32),
    )
    block_input_gradient = lax.all_to_all(
        input_sum.astype(jnp.bfloat16), "dp", split_axis=0, concat_axis=2, tiled=True
    )
    rank_own = lax.dynamic_slice_in_dim(rank_sum, group_index, 1, 0)[0]
    down_map_terms = jnp.dot(
        rank_own.T, inputs[0].astype(jnp.float32), precision=lax.Precision.HIGHEST
    )
    down_map_total = lax.psum(down_map_terms, ("dp", "tensor"))
    adapter_down_gradient = (down_map_total * gradient_scale).reshape(
        2, adapter_rank_count, width_of_model
    )
    return (block_input_gradient, adapter_down_gradient, adapter_up_gradient)


def solution(mesh):
    placed = (
        P("dp", "tensor", None),
        P("dp", "tensor", None),
        P("dp", None, "tensor"),
        P("dp", None, "tensor"),
        P("dp", "tensor"),
        P("dp", "tensor"),
        P("tensor", "dp"),
        P(),
        P(None, None, "tensor"),
    )
    return jax.shard_map(
        on_device,
        mesh=mesh,
        in_specs=placed,
        out_specs=(P("dp", "tensor", None), P(), P(None, None, "tensor")),
        check_vma=False,
    )
```

profile of v0, /device:TPU:1, one launch (start us, length us, event | category | flops | bytes accessed | tf_op | source)
XLA Modules:
  0.0 737.7 jit_solution(5359474628701258277)
XLA Ops:
  7.2 1.5 fusion.9
  9.0 12.7 %copy.26 = bf16[1,8,16384]{1,0,2:T(2,128)(2,1)} copy(bf16[1,8,16384]{2,1,0:T(8,128)(2,1)S(1)} %convert_element_type.71) | data formatting | bytes 524288 | tf_op jit(solution)/shard_map/convert_element_type | solution.py:27
  22.2 90.8 %reduce = bf16[16384,8]{1,0:T(8,128)(2,1)} reduce(bf16[16384,1,8]{2,1,0:T(2,128)(2,1)} %bitcast.81, bf16[]{:T(256)} %broadcast.108), dimensions={1}, to_apply=%bitcast.72.reduce_sub_computation | reduce | bytes 524290
  113.0 5.8 reshape.71
  118.8 13.1 %all_to_all.36 = bf16[8,2,8192]{2,1,0:T(2,128)(2,1)S(1)} all-to-all(bf16[8,2,8192]{2,1,0:T(2,128)(2,1)S(1)} %reshape.71), channel_id=1, replica_groups=mesh['dp'=8,'tensor'=16] {'dp'}, dimensions={0} | all-to-all | bytes 524288 | tf_op jit(solution)/shard_map/all_to_all | solution.py:67
  131.9 10.9 %reshape.72 = bf16[16384,1,8]{2,1,0:T(2,128)(2,1)} reshape(bf16[8,2,8192]{2,1,0:T(2,128)(2,1)S(1)} %all_to_all.36) | data formatting | bytes 524288
  142.7 16.0 %copy.27 = bf16[1,8,16384]{2,1,0:T(8,128)(2,1)} copy(bf16[1,8,16384]{1,0,2:T(2,128)(2,1)} %bitcast.82) | data formatting | bytes 524288 | tf_op jit(solution)/shard_map/all_to_all | solution.py:67
  159.0 51.3 %all-gather.10.cloned.1.call-done = bf16[8,1,128,2048]{3,2,0,1:T(8,128)(2,1)} async-done(((bf16[8,1,8,2048]{3,2,0,1:T(8,128)(2,1)}), bf16[8,1,128,2048]{3,2,0,1:T(8,128)(2,1)}) %all-gather.10.cloned.1.call-update) | async-done | bytes 4194320 | tf_op jit(solution)/shard_map/all_gather | solution.py:69
  210.2 13.3 %fusion.4 = f32[8,128,1664]{2,1,0:T(8,128)} fusion(bf16[1664,2048]{1,0:T(8,128)(2,1)} %param.15, bf16[8,1,128,2048]{3,2,0,1:T(8,128)(2,1)} %all-gather.10.cloned.1.call-done), kind=kOutput, calls=%fused_computation.5 | convolution fusion | flops 6979321856 | bytes 17825792 | tf_op jit(solution)/shard_map/dot_general | solution.py:42
  223.6 44.3 %reduce-scatter.4.cloned.1.call-done = f32[1,128,1664]{2,1,0:T(8,128)} async-done(((f32[8,128,1664]{2,1,0:T(8,128)}), f32[1,128,1664]{2,1,0:T(8,128)}) %reduce-scatter.4.cloned.1.call-update) | async-done | bytes 851984 | tf_op jit(solution)/shard_map/reduce_scatter | solution.py:76
  267.9 2.5 fusion.18
  272.1 19.0 %all-gather.1 = bf16[128,32]{1,0:T(8,128)(2,1)S(1)} all-gather(bf16[8,32]{1,0:T(8,128)(2,1)S(1)} %convolution_convert_fusion.4), channel_id=3, replica_groups=mesh['dp'=8,'tensor'=16] {'tensor'}, dimensions={0}, use_global_device_ids=true | all-gather | bytes 8704 | tf_op jit(solution)/shard_map/all_gather | solution.py:70
  291.1 1.2 fusion.7
  292.6 7.6 %all-gather.8.cloned.1.call-done = bf16[8,128,1664]{2,1,0:T(8,128)(2,1)} async-done(((bf16[1,128,1664]{2,1,0:T(8,128)(2,1)}), bf16[8,128,1664]{2,1,0:T(8,128)(2,1)}) %all-gather.8.cloned.1.call-update) | async-done | bytes 3407888 | tf_op jit(solution)/shard_map/all_gather | solution.py:80
  300.2 2.9 fusion.39
  303.1 27.4 %all-gather.6.cloned.1.call-done = bf16[8,128,1664]{2,1,0:T(8,128)(2,1)} async-done(((bf16[1,128,1664]{2,1,0:T(8,128)(2,1)}), bf16[8,128,1664]{2,1,0:T(8,128)(2,1)}) %all-gather.6.cloned.1.call-update) | async-done | bytes 3407888 | tf_op jit(solution)/shard_map/all_gather | solution.py:79
  330.6 2.9 fusion.41
  333.6 0.9 copy.29
  335.5 11.1 %fusion = f32[8,128,2048]{2,1,0:T(8,128)S(1)} fusion(bf16[8,128,1664]{2,1,0:T(8,128)(2,1)} %all-gather.8.cloned.1.call-done, bf16[2048,1664]{1,0:T(8,128)(2,1)} %param.14), kind=kOutput, calls=%fused_computation.1 | convolution fusion | flops 6979321856 | bytes 18612224 | tf_op jit(solution)/shard_map/dot_general | solution.py:42
  346.6 10.0 %fusion.2 = f32[8,128,2048]{2,1,0:T(8,128)S(1)} fusion(bf16[8,128,1664]{2,1,0:T(8,128)(2,1)S(1)} %copy-done.2, bf16[2048,1664]{1,0:T(8,128)(2,1)} %param.13), kind=kOutput, calls=%fused_computation.3 | convolution fusion | flops 6979321856 | bytes 18612224 | tf_op jit(solution)/shard_map/dot_general | solution.py:42
  356.6 5.6 add_convert_fusion
  362.3 42.0 %reduce-scatter.6.cloned.1.call-done = bf16[8,8,32]{2,0,1:T(8,128)(2,1)} async-done(((bf16[8,128,32]{2,0,1:T(8,128)(2,1)}), bf16[8,8,32]{2,0,1:T(8,128)(2,1)}) %reduce-scatter.6.cloned.1.call-update) | async-done | bytes 4112 | tf_op jit(solution)/shard_map/reduce_scatter | solution.py:122
  404.2 0.7 constant_dynamic-slice_fusion.1
  405.0 1.8 fusion.22
  408.0 57.3 %all-reduce.7.cloned.1.call-done = bf16[2,16,1664]{2,1,0:T(8,128)(2,1)} async-done(((bf16[2,16,1664]{2,1,0:T(8,128)(2,1)}), bf16[2,16,1664]{2,1,0:T(8,128)(2,1)}) %all-reduce.7.cloned.1.call-update) | async-done | bytes 106512 | tf_op jit(solution)/shard_map/psum | solution.py:97
  465.4 1.6 convert_multiply_fusion.2
  466.9 104.4 %all-reduce.9.cloned.1.call-done = bf16[8,128,2048]{2,1,0:T(8,128)(2,1)} async-done(((bf16[8,128,2048]{2,1,0:T(8,128)(2,1)}), bf16[8,128,2048]{2,1,0:T(8,128)(2,1)}) %all-reduce.9.cloned.1.call-update) | async-done | bytes 4194320
  571.4 1.7 constant_dynamic-slice_fusion
  573.0 5.3 all-to-all-start.1
  578.3 148.8 %all-reduce.5.cloned.1.call-done = f32[32,16384]{1,0:T(8,128)} async-done(((f32[32,16384]{1,0:T(8,128)}), f32[32,16384]{1,0:T(8,128)}) %all-reduce.5.cloned.1.call-update) | async-done | bytes 2097168 | tf_op jit(solution)/shard_map/psum | solution.py:133
  727.1 3.0 broadcast_multiply_fusion
  730.2 0.7 copy.55
  (43 shorter events, 4.8 us)
Async XLA Ops:
  7.2 264.5 %copy-start = (bf16[2,16,16384]{2,1,0:T(8,128)(2,1)S(1)}, bf16[2,16,16384]{2,1,0:T(8,128)(2,1)}, u32[]{:S(2)}) copy-start(bf16[2,16,16384]{2,1,0:T(8,128)(2,1)} %param.16) | copy-start | bytes 3145732
  7.2 203.1 %all-gather.10.cloned.1.call-start = ((), (), s32[]{:S(2)}) async-start(), calls=%async_computation.10 | async-start | bytes 4456448 | tf_op jit(solution)/shard_map/all_gather | solution.py:69
  158.7 109.2 %reduce-scatter.4.cloned.1.call-start = ((), (), s32[]{:S(2)}) async-start(), calls=%async_computation.4 | async-start | bytes 7667712 | tf_op jit(solution)/shard_map/reduce_scatter | solution.py:76
  223.5 44.4 %copy-start.3 = (bf16[1,128,1664]{2,1,0:T(8,128)(2,1)S(1)}, bf16[1,128,1664]{2,1,0:T(8,128)(2,1)}, u32[]{:S(2)}) copy-start(bf16[1,128,1664]{2,1,0:T(8,128)(2,1)} %param.11) | copy-start | bytes 1277956
  223.5 44.4 %copy-start.4 = (bf16[1,128,1664]{2,1,0:T(8,128)(2,1)S(1)}, bf16[1,128,1664]{2,1,0:T(8,128)(2,1)}, u32[]{:S(2)}) copy-start(bf16[1,128,1664]{2,1,0:T(8,128)(2,1)} %param.12) | copy-start | bytes 1277956
  223.5 47.5 %copy-start.6 = (bf16[1,8,16384]{2,1,0:T(8,128)(2,1)S(1)}, bf16[1,8,16384]{2,1,0:T(8,128)(2,1)}, u32[]{:S(2)}) copy-start(bf16[1,8,16384]{2,1,0:T(8,128)(2,1)} %param.9) | copy-start | bytes 786436
  223.6 76.7 %copy-start.5 = (bf16[2,16,1664]{2,1,0:T(8,128)(2,1)S(1)}, bf16[2,16,1664]{2,1,0:T(8,128)(2,1)}, u32[]{:S(2)}) copy-start(bf16[2,16,1664]{2,1,0:T(8,128)(2,1)} %param.17) | copy-start | bytes 319492
  223.6 76.6 %all-gather.8.cloned.1.call-start = ((), (), s32[]{:S(2)}) async-start(), calls=%async_computation.6 | async-start | bytes 3833856 | tf_op jit(solution)/shard_map/all_gather | solution.py:80
  270.4 21.9 %copy-start.1 = (bf16[1,128,1664]{2,1,0:T(8,128)(2,1)S(1)}, bf16[1,128,1664]{2,1,0:T(8,128)(2,1)}, u32[]{:S(2)}) copy-start(bf16[1,128,1664]{2,1,0:T(8,128)(2,1)} %get-tuple-element.3) | copy-start | bytes 1277956
  270.4 60.2 %all-gather.6.cloned.1.call-start = ((), (), s32[]{:S(2)}) async-start(), calls=%async_computation.5 | async-start | bytes 3833856 | tf_op jit(solution)/shard_map/all_gather | solution.py:79
  271.0 133.2 %reduce-scatter.6.cloned.1.call-start = ((), (), s32[]{:S(2)}) async-start(), calls=%async_computation.7 | async-start | bytes 278528 | tf_op jit(solution)/shard_map/reduce_scatter | solution.py:122
  334.5 130.9 %all-reduce.7.cloned.1.call-start = ((), (), s32[]{:S(2)}) async-start(), calls=%async_computation.9 | async-start | bytes 212992 | tf_op jit(solution)/shard_map/psum | solution.py:97
  335.2 236.2 %all-reduce.9.cloned.1.call-start = ((), (), s32[]{:S(2)}) async-start(), calls=%async_computation.11 | async-start | bytes 8388608
  335.5 11.2 %copy-start.2 = (bf16[8,128,1664]{2,1,0:T(8,128)(2,1)S(1)}, bf16[8,128,1664]{2,1,0:T(8,128)(2,1)}, u32[]{:S(2)}) copy-start(bf16[8,128,1664]{2,1,0:T(8,128)(2,1)} %all-gather.6.cloned.1.call-done) | copy-start | bytes 10223620
  362.2 44.6 %copy-start.7 = (u32[128]{0:T(128)S(1)}, u32[128]{0:T(128)}, u32[]{:S(2)}) copy-start(u32[128]{0:T(128)} %constant.58) | copy-start | bytes 1540
  362.2 364.9 %all-reduce.5.cloned.1.call-start = ((), (), s32[]{:S(2)}) async-start(), calls=%async_computation.8 | async-start | bytes 4194304 | tf_op jit(solution)/shard_map/psum | solution.py:133
  573.0 157.2 %all-to-all-start.1 = ((bf16[8,8,2048]{2,1,0:T(8,128)(2,1)}), bf16[8,8,2048]{2,1,0:T(8,128)(2,1)S(1)}, u32[]{:S(2)}, u32[]{:S(2)}) async-start(bf16[8,8,2048]{2,1,0:T(8,128)(2,1)} %constant_dynamic-slice_fusion), calls=%async_computation.2 | async-start | bytes 524288 | tf_op jit(solution)/shard_map/all_to_all | solution.py:126
Sparse Core Ops, SparseCore 0:
  158.9 51.3 all-gather.9
  223.7 44.1 reduce-scatter.3
  270.5 29.6 all-gather.7
  301.7 28.7 all-gather.5
  334.6 69.5 reduce-scatter.5
  407.1 58.2 all-reduce.6
  468.7 102.6 all-reduce.8
  576.8 150.3 all-reduce.4
where the time goes:
time: 739 us; the launch traced here: 738 us
  waiting for transfers between devices  484 us (65%)
  other arithmetic  98.6 us (13%)
  matrix products  51.4 us (7%)
  local copies, waits for them, and re-layouts  50.9 us (7%)
  blocking collectives  32.1 us (4%)
  between operations  14.9 us (2%)
    psum x1, waiting for transfers between devices, on_device(): down_map_total = lax.psum(down_map_terms, ('dp', 'tensor'))  149 us
    unnamed x9, waiting for transfers between devices  105 us
    unnamed x1, other arithmetic  90.8 us
    psum x1, waiting for transfers between devices, on_device(): lax.psum(jnp.stack([gate_up_map, up_branch_map]).astype(jnp.bfloat16), 'dp')  57.3 us
    all_gather x1, waiting for transfers between devices, on_device(): lax.all_gather(grad_split, 'tensor', axis=1, tiled=True)  51.3 us
    reduce_scatter x1, waiting for transfers between devices, on_device(): lax.psum_scatter(hidden_part, 'dp', scatter_dimension=0, tiled=True)  44.3 us
    reduce_scatter x1, waiting for transfers between devices, on_device(): lax.psum_scatter(rank_part.astype(jnp.bfloat16), 'tensor', scatter_dimens...  42 us
    dot_general x5, matrix products, contract_trailing(): lax.dot_general(left, right, (((2,), (1,)), ((), ())), preferred_element_...  40.3 us
  transfers between devices with their start and end apart: 9, of which 8 were waited for; matrix products, arithmetic and copies ran while one was open for 6% of the time, Pallas kernels for 0%

commit v1 on v0

v1 whole, which is shorter than its diff:
```python
import functools

import jax
import jax.numpy as jnp
import numpy as np
from jax import lax
from jax.experimental import pallas as pl
from jax.experimental.pallas import tpu as pltpu
from jax.sharding import PartitionSpec as P

F32 = jnp.float32
BF16 = jnp.bfloat16
HB = 128
WIDTH = 16384
SLICE = 2048
HALF = 1024
HID = 1664
RANK = 16
SCALE = 2.0
GRAD_SCALE = SCALE / 1024.0**0.5
ORDER1 = (2, 1, 3, 0)
ORDER2 = (0, 3, 1, 2)
TILES1 = ((0, 640), (640, 512), (1152, 512))
TILE2 = 512
NSEM = 264
NT = (((1,), (1,)), ((), ()))


def sign_table():
    index = np.arange(HB)
    common = index[:, None] & index[None, :]
    parity = np.zeros_like(common)
    for bit in range(7):
        parity += (common >> bit) & 1
    return (1 - 2 * (parity % 2)).astype(np.float32)


def kernel(
    x_ref, dy_ref, g_ref, u_ref, am_ref, um_ref, h_ref, wd_hbm, wg_hbm, wu_hbm,
    out_ref, down_ref, up_ref,
    wd, wg, wu, s_buf, r_buf, y_buf, xg, p_buf, q_buf, f_buf, gz_buf, d_buf, ab, o_buf,
    r1, r2, r3, r4, t_buf, v_buf, ad_s, ad_r, adn, zs, zr, ds_buf, dr_buf, e_buf, a_own, u_pad,
    ss, rs, ws,
):
    d = lax.axis_index("dp")
    t = lax.axis_index("tensor")
    z, c = d // 2, d % 2
    oc = 1 - c
    pos = {"y": t // 4, "x": t % 4}
    count = [0]
    pending = []

    def unit(k):
        return (z + k) % 4

    zp, zm = unit(1), unit(3)
    sib = (z * 2 + oc, t)
    up_dev, down_dev = (zp * 2 + c, t), (zm * 2 + c, t)

    def near(axis, k):
        moved = dict(pos)
        moved[axis] = (pos[axis] + k) % 4
        return (d, moved["y"] * 4 + moved["x"])

    def send(src, dst, dev):
        k = count[0]
        count[0] += 1
        copy = pltpu.make_async_remote_copy(
            src_ref=src, dst_ref=dst, send_sem=ss.at[k], recv_sem=rs.at[k],
            device_id=dev, device_id_type=pl.DeviceIdType.MESH,
        )
        copy.start()
        pending.append(copy)
        return k, copy

    def arrived(k, dst):
        pltpu.make_async_remote_copy(
            src_ref=dst, dst_ref=dst, send_sem=ss.at[k], recv_sem=rs.at[k],
            device_id=sib, device_id_type=pl.DeviceIdType.MESH,
        ).wait_recv()

    def sent(copy):
        copy.wait_send()
        pending[:] = [other for other in pending if other is not copy]

    loads = []
    for k, (src, dst) in enumerate(((wd_hbm, wd), (wg_hbm, wg), (wu_hbm, wu))):
        copy = pltpu.make_async_copy(src, dst, ws.at[k])
        copy.start()
        loads.append(copy)

    barrier = pltpu.get_barrier_semaphore()
    for i in range(1, 8):
        pl.semaphore_signal(barrier, inc=1, device_id=((d + i) % 8, t), device_id_type=pl.DeviceIdType.MESH)
    for i in range(1, 16):
        pl.semaphore_signal(barrier, inc=1, device_id=(d, (t + i) % 16), device_id_type=pl.DeviceIdType.MESH)

    def rotate(src, slot):
        flat = src[0].astype(F32)
        rows = jnp.concatenate([flat[:, HB * k : HB * (k + 1)] for k in range(WIDTH // HB)], axis=0)
        turned = jnp.dot(rows.astype(BF16), h_ref[...], preferred_element_type=F32) * (1.0 / HB**0.5)
        for p in range(8):
            for j in range(8):
                first, second = 8 * (16 * p + j), 8 * (16 * p + 8 + j)
                s_buf[slot, p, :, HB * j : HB * (j + 1)] = jnp.concatenate(
                    [turned[first : first + 8], turned[second : second + 8]], axis=0
                ).astype(BF16)

    rels = [(k, o) for k in (2, 1, 3, 0) for o in (0, 1) if (k, o) != (0, 0)]

    def peer(k, o):
        return unit(k) * 2 + (oc if o else c)

    def source(k, o):
        return unit((4 - k) % 4) * 2 + (oc if o else c)

    rotate(dy_ref, 0)
    pl.semaphore_wait(barrier, 22)
    first_a2a = {}
    for slot in range(2):
        if slot == 1:
            rotate(x_ref, 1)
        for k, o in rels:
            first_a2a[slot, k, o] = send(
                s_buf.at[slot, peer(k, o)], r_buf.at[slot, d], (peer(k, o), t)
            )[0]
        r_buf[slot, d] = s_buf[slot, d]

    def factors(i, carry):
        rows = pl.ds(pl.multiple_of(i * 16, 16), 16)
        gate = g_ref[0, rows, :].astype(F32)
        up = u_ref[0, rows, :].astype(F32)
        squash = 1.0 / (1.0 + jnp.exp(-gate))
        ab[z, 0, c, rows, :] = (up * squash * (1.0 + gate * (1.0 - squash))).astype(BF16)
        ab[z, 1, c, rows, :] = (gate * squash).astype(BF16)
        return carry

    lax.fori_loop(0, 8, factors, 0)

    class ZGather:
        def __init__(self, whole, half):
            self.whole, self.half = whole, half
            self.copies = {0: [], 1: [], 2: [], 3: []}
            self.k_from = {}

        def begin(self):
            self.k_up = self.push(0, self.whole(z, c), up_dev)
            self.k_down = self.push(0, self.whole(z, c), down_dev)
            self.k_from[0] = self.push(0, self.whole(z, c), sib)

        def push(self, owner, ref, dev):
            k, copy = send(ref, ref, dev)
            self.copies[owner].append(copy)
            return k

        def onward(self):
            arrived(self.k_up, self.whole(zm, c))
            self.k_f0 = self.push(3, self.half(zm, c, 0), up_dev)
            self.k_from[3] = self.push(3, self.whole(zm, c), sib)
            arrived(self.k_down, self.whole(zp, c))
            self.k_f1 = self.push(1, self.half(zp, c, 1), down_dev)
            self.k_from[1] = self.push(1, self.whole(zp, c), sib)

        def last(self):
            arrived(self.k_f0, self.half(unit(2), c, 0))
            arrived(self.k_f1, self.half(unit(2), c, 1))
            self.k_from[2] = self.push(2, self.whole(unit(2), c), sib)

        def have(self, rel):
            arrived(self.k_from[rel], self.whole(unit(rel), oc))

        def release(self, rel):
            for copy in self.copies[rel]:
                sent(copy)

    ab_gather = ZGather(
        lambda u, core: ab.at[u, :, core],
        lambda u, core, i: ab.at[u, i, core],
    )
    ab_gather.begin()

    def unpack(slot, u):
        low = r_buf[slot, 2 * u].astype(F32)
        high = r_buf[slot, 2 * u + 1].astype(F32)
        left = jnp.concatenate([low[:8], high[:8]], axis=0).astype(BF16)
        right = jnp.concatenate([low[8:], high[8:]], axis=0).astype(BF16)
        return left, right

    for k, o in rels:
        arrived(first_a2a[0, k, o], r_buf.at[0, source(k, o)])
    for i, rel in enumerate(ORDER1):
        left, right = unpack(0, unit(rel))
        y_buf[i, pos["y"], pos["x"], :, :HALF] = left
        y_buf[i, pos["y"], pos["x"], :, HALF:] = right

    AXES = (("x", "y"), ("y", "x"))

    def block(buf, lead, h, f, g, cols):
        yy, xx = (g, f) if AXES[h][0] == "x" else (f, g)
        return buf.at[lead, yy, xx, :, cols]

    COLS = (pl.ds(0, HALF), pl.ds(HALF, HALF))
    chunks = ((0, 2), (2, 2))
    keys = {}

    def shift(axis, k):
        return (pos[axis] + k) % 4

    def lead_of(n, part):
        start, size = chunks[n]
        if part == "all":
            return pl.ds(start, size)
        return pl.ds(start, size // 2) if part == "first" else pl.ds(start + size // 2, size // 2)

    def ag1_ref(n, h, fr, part):
        f_axis, g_axis = AXES[h]
        return block(y_buf, lead_of(n, part), h, shift(f_axis, fr), pos[g_axis], COLS[h])

    def ag2_ref(n, h, fr, gr, part):
        f_axis, g_axis = AXES[h]
        return block(y_buf, lead_of(n, part), h, shift(f_axis, fr), shift(g_axis, gr), COLS[h])

    def ag_push(key, ref, axis, k):
        keys[key] = send(ref, ref, near(axis, k))[0]

    def stage2_own(n, h, fr):
        g_axis = AXES[h][1]
        for k in (1, -1):
            ag_push(("2", n, h, fr, k), ag2_ref(n, h, fr, 0, "all"), g_axis, k)

    def stage2_onward(n, h, fr):
        g_axis = AXES[h][1]
        for k, part in ((1, "first"), (-1, "second")):
            arrived(keys["2", n, h, fr, k], ag2_ref(n, h, fr, -k, "all"))
            ag_push(("2f", n, h, fr, k), ag2_ref(n, h, fr, -k, part), g_axis, k)

    def ag_step0(n):
        for h in (0, 1):
            for k in (1, -1):
                ag_push(("1", n, h, k), ag1_ref(n, h, 0, "all"), AXES[h][0], k)
            stage2_own(n, h, 0)

    def ag_step1(n):
        for h in (0, 1):
            for k, part in ((1, "first"), (-1, "second")):
                arrived(keys["1", n, h, k], ag1_ref(n, h, -k, "all"))
                ag_push(("1f", n, h, k), ag1_ref(n, h, -k, part), AXES[h][0], k)
                stage2_own(n, h, -k)

    def ag_step2(n):
        for h in (0, 1):
            for k, part in ((1, "first"), (-1, "second")):
                arrived(keys["1f", n, h, k], ag1_ref(n, h, 2, part))
            stage2_own(n, h, 2)
            stage2_onward(n, h, 0)

    def ag_step3(n):
        for h in (0, 1):
            for fr in (-1, 1):
                stage2_onward(n, h, fr)

    def ag_step4(n):
        for h in (0, 1):
            stage2_onward(n, h, 2)

    def ag_step5(n):
        for h in (0, 1):
            for fr in (0, -1, 1, 2):
                for k, part in ((1, "first"), (-1, "second")):
                    arrived(keys["2f", n, h, fr, k], ag2_ref(n, h, fr, 2, part))

    ag_step0(0)
    ag_step0(1)

    a_own[...] = am_ref[:, :, pl.ds(pl.multiple_of(d * SLICE, SLICE), SLICE)].reshape(2 * RANK, SLICE)
    u_pad[0, :RANK] = um_ref[0]
    u_pad[1, RANK:] = um_ref[1]
    u_pad[0, RANK:] = jnp.zeros((RANK, HID), BF16)
    u_pad[1, :RANK] = jnp.zeros((RANK, HID), BF16)
    zs[...] = jnp.zeros_like(zs)
    ad_s[...] = jnp.zeros_like(ad_s)
    tops = jnp.zeros((16, 2 * RANK), F32)
    bottoms = jnp.zeros((16, 2 * RANK), F32)
    for p in range(8):
        tokens = s_buf[1, p]
        for part in range(2):
            start = p * SLICE + part * HALF
            maps = am_ref[:, :, start : start + HALF].reshape(2 * RANK, HALF)
            value = lax.dot_general(tokens, maps, NT, preferred_element_type=F32)
            if part == 0:
                tops = tops + value
            else:
                bottoms = bottoms + value
    ad_s[:, : 2 * RANK] = jnp.concatenate([tops[:8] + bottoms[8:], jnp.zeros((8, 2 * RANK), F32)], axis=0).astype(BF16)

    ag_step1(0)
    ag_step1(1)

    ad_keys = {}
    for k, o in rels:
        ad_keys[k, o] = send(ad_s, ad_r.at[d], (peer(k, o), t))[0]
    ad_r[d] = ad_s[...]
    for k, o in rels:
        arrived(first_a2a[1, k, o], r_buf.at[1, source(k, o)])
    for u in range(4):
        left, right = unpack(1, u)
        xg[u, :, :HALF] = left
        xg[u, :, HALF:] = right

    ag_step2(0)
    ag_step2(1)
    for k, o in rels:
        arrived(ad_keys[k, o], ad_r.at[source(k, o)])
    for u in range(4):
        adn[t, u] = jnp.concatenate(
            [ad_r[2 * u].astype(F32)[:8], ad_r[2 * u + 1].astype(F32)[:8]], axis=0
        ).astype(BF16)
    adt_keys = {}
    for i in range(1, 16):
        adt_keys[i] = send(adn.at[t], adn.at[t], (d, (t + i) % 16))[0]
    ag_step3(0)
    ag_step3(1)
    ab_gather.onward()
    ag_step4(0)
    ag_step4(1)

    loads[0].wait()
    core_keys = {}

    def product1(i):
        rows = y_buf[i].reshape(256, SLICE)
        for start, size in TILES1:
            value = lax.dot_general(
                rows, wd[start : start + size, :], NT, preferred_element_type=F32
            ).reshape(16, 2, 8, size)
            for core in range(2):
                p_buf[i, core, :, start : start + size] = value[:, core].reshape(128, size).astype(BF16)
        core_keys[i] = send(p_buf.at[i, oc], q_buf.at[i], sib)[0]

    def add_rows(dst, others, lo=0, hi=128):
        def body(i, carry):
            value = None
            rows = pl.ds(pl.multiple_of(lo + i * 16, 16), 16)
            value = dst[0][rows, :].astype(F32)
            for ref, base in others:
                here = pl.ds(pl.multiple_of(lo - base + i * 16, 16), 16)
                value = value + ref[here, :].astype(F32)
            dst[1][rows, :] = value.astype(BF16)
            return carry

        lax.fori_loop(0, (hi - lo) // 16, body, 0)

    ag_step5(0)
    product1(0)
    product1(1)
    ag_step5(1)
    own = [p_buf.at[i, c] for i in range(4)]
    arrived(core_keys[0], q_buf.at[0])
    add_rows((own[0], own[0]), [(q_buf.at[0], 0)])
    k_f0 = send(p_buf.at[0, c, pl.ds(0, 64)], f_buf.at[0], up_dev)[0]
    k_f1 = send(p_buf.at[0, c, pl.ds(64, 64)], f_buf.at[1], down_dev)[0]
    product1(2)
    arrived(core_keys[1], q_buf.at[1])
    arrived(k_f0, f_buf.at[0])
    add_rows((own[1], own[1]), [(q_buf.at[1], 0), (f_buf.at[0], 0)], 0, 64)
    add_rows((own[1], own[1]), [(q_buf.at[1], 0)], 64, 128)
    k_g0 = send(p_buf.at[1, c], gz_buf.at[0], up_dev)[0]
    arrived(core_keys[2], q_buf.at[2])
    arrived(k_f1, f_buf.at[1])
    add_rows((own[2], own[2]), [(q_buf.at[2], 0)], 0, 64)
    add_rows((own[2], own[2]), [(q_buf.at[2], 0), (f_buf.at[1], 64)], 64, 128)
    k_g1 = send(p_buf.at[2, c], gz_buf.at[1], down_dev)[0]
    product1(3)
    ab_gather.last()
    ab_gather.have(0)
    ab_gather.have(3)
    ab_gather.have(1)
    for i in range(1, 16):
        arrived(adt_keys[i], adn.at[(t + 16 - i) % 16])
    arrived(core_keys[3], q_buf.at[3])
    arrived(k_g0, gz_buf.at[0])
    arrived(k_g1, gz_buf.at[1])
    add_rows((own[3], d_buf.at[z, c]), [(q_buf.at[3], 0), (gz_buf.at[0], 0), (gz_buf.at[1], 0)])

    d_gather = ZGather(
        lambda u, core: d_buf.at[u, core],
        lambda u, core, i: d_buf.at[u, core, pl.ds(64 * i, 64)],
    )
    d_gather.begin()
    loads[1].wait()
    loads[2].wait()

    rs_keys = {}

    def gradients(rel):
        u = unit(rel)
        ab_gather.release(rel)
        for core in range(2):

            def body(i, carry):
                rows = pl.ds(pl.multiple_of(i * 16, 16), 16)
                hidden = d_buf[u, core, rows, :].astype(F32)
                ab[u, 0, core, rows, :] = (hidden * ab[u, 0, core, rows, :].astype(F32)).astype(BF16)
                ab[u, 1, core, rows, :] = (hidden * ab[u, 1, core, rows, :].astype(F32)).astype(BF16)
                return carry

            lax.fori_loop(0, 8, body, 0)

    def by_token(value):
        pieces = []
        for i in range(16):
            pieces += [value[8 * i : 8 * i + 8], value[128 + 8 * i : 136 + 8 * i]]
        return jnp.concatenate(pieces, axis=0)

    def rank_terms(rel):
        u = unit(rel)
        gate = ab[u, 0].reshape(256, HID)
        up = ab[u, 1].reshape(256, HID)
        ranks = lax.dot_general(gate, u_pad[0], NT, preferred_element_type=F32) + lax.dot_general(
            up, u_pad[1], NT, preferred_element_type=F32
        )
        zs[:, u, :, : 2 * RANK] = by_token(ranks).astype(BF16).reshape(16, 16, 2 * RANK)
        return (SCALE * ranks).astype(BF16)

    def product2(rel, ranks):
        u = unit(rel)

        def body(n, carry):
            rows = pl.ds(pl.multiple_of(n * TILE2, TILE2), TILE2)
            value = lax.dot_general(ab[u, 0].reshape(256, HID), wg[rows, :], NT, preferred_element_type=F32)
            value = value + lax.dot_general(ab[u, 1].reshape(256, HID), wu[rows, :], NT, preferred_element_type=F32)
            value = value + jnp.dot(ranks, a_own[:, rows], preferred_element_type=F32)
            o_buf[u, :, :, :, rows] = by_token(value).astype(BF16).reshape(4, 4, 16, TILE2)
            return carry

        lax.fori_loop(0, SLICE // TILE2, body, 0)

    RAXES = (("y", "x"), ("x", "y"))

    def out_block(u, h, f, g, cols):
        yy, xx = (f, g) if RAXES[h][0] == "y" else (g, f)
        return o_buf.at[u, yy, xx, :, cols]

    def add_into(dst, src):
        dst[...] = (dst[...].astype(F32) + src[...].astype(F32)).astype(BF16)

    def rs_step1(rel):
        u = unit(rel)
        for h in (0, 1):
            f_axis = RAXES[h][0]
            for i, k in enumerate((1, -1)):
                rs_keys["1", rel, h, k] = send(
                    out_block(u, h, shift(f_axis, 2), pl.ds(2 * i, 2), COLS[h]),
                    r1.at[u, h, i],
                    near(f_axis, k),
                )[0]

    def rs_step2(rel):
        u = unit(rel)
        for h in (0, 1):
            f_axis = RAXES[h][0]
            for i, k in enumerate((1, -1)):
                arrived(rs_keys["1", rel, h, k], r1.at[u, h, i])
                for j in range(2):
                    add_into(out_block(u, h, shift(f_axis, k), 2 * i + j, COLS[h]), r1.at[u, h, i, j])
                rs_keys["2", rel, h, k] = send(
                    out_block(u, h, shift(f_axis, k), pl.ds(0, 4), COLS[h]),
                    r2.at[u, h, i],
                    near(f_axis, k),
                )[0]

    def half_cols(h, i):
        return pl.ds(HALF * h + 512 * i, 512)

    def rs_step3(rel):
        u = unit(rel)
        for h in (0, 1):
            f_axis, g_axis = RAXES[h]
            for i, k in enumerate((1, -1)):
                arrived(rs_keys["2", rel, h, k], r2.at[u, h, i])
            for j in range(4):
                dst = out_block(u, h, pos[f_axis], j, COLS[h])
                dst[...] = (
                    dst[...].astype(F32) + r2[u, h, 0, j].astype(F32) + r2[u, h, 1, j].astype(F32)
                ).astype(BF16)
            for i, k in enumerate((1, -1)):
                rs_keys["3", rel, h, k] = send(
                    out_block(u, h, pos[f_axis], shift(g_axis, 2), half_cols(h, i)),
                    r3.at[u, h, i],
                    near(g_axis, k),
                )[0]

    def rs_step4(rel):
        u = unit(rel)
        for h in (0, 1):
            f_axis, g_axis = RAXES[h]
            for i, k in enumerate((1, -1)):
                arrived(rs_keys["3", rel, h, k], r3.at[u, h, i])
                add_into(out_block(u, h, pos[f_axis], shift(g_axis, k), half_cols(h, i)), r3.at[u, h, i])
                rs_keys["4", rel, h, k] = send(
                    out_block(u, h, pos[f_axis], shift(g_axis, k), COLS[h]),
                    r4.at[u, h, i],
                    near(g_axis, k),
                )[0]

    last_a2a = {}

    def rs_step5(rel):
        u = unit(rel)
        halves = []
        for h in (0, 1):
            f_axis, g_axis = RAXES[h]
            for i, k in enumerate((1, -1)):
                arrived(rs_keys["4", rel, h, k], r4.at[u, h, i])
            own_block = out_block(u, h, pos[f_axis], pos[g_axis], COLS[h])[...].astype(F32)
            halves.append(own_block + r4[u, h, 0].astype(F32) + r4[u, h, 1].astype(F32))
        for core in range(2):
            rows = slice(8 * core, 8 * core + 8)
            t_buf[2 * u + core] = jnp.concatenate([halves[0][rows], halves[1][rows]], axis=0).astype(BF16)
        for o in (0, 1):
            if (rel, o) == (0, 0):
                v_buf[d] = t_buf[d]
            else:
                last_a2a[rel, o] = send(t_buf.at[peer(rel, o)], v_buf.at[d], (peer(rel, o), t))[0]

    steps = (rs_step1, rs_step2, rs_step3, rs_step4, rs_step5)

    def advance(turn):
        for s in range(5):
            i = turn - s
            if 0 <= i < 4:
                steps[s](ORDER2[i])

    def z_sum():
        for i in range(1, 16):
            arrived(z_keys[i], zr.at[(t + 16 - i) % 16])
        zr[t] = zs[t]
        total = zr[0].astype(F32)
        for i in range(1, 16):
            total = total + zr[i].astype(F32)
        turned = jnp.transpose(total.reshape(64, 128))[: 2 * RANK].astype(BF16)
        terms = jnp.dot(turned, xg[...].reshape(64, SLICE), preferred_element_type=F32)
        for i in range(16):
            ds_buf[i] = terms[:, HB * i : HB * (i + 1)].astype(BF16)
        for i in range(1, 16):
            to = (t + i) % 16
            down_keys[i] = send(ds_buf.at[to], dr_buf.at[t], (d, to))[0]
        dr_buf[t] = ds_buf[t]

    def down_sum():
        for i in range(1, 16):
            arrived(down_keys[i], dr_buf.at[(t + 16 - i) % 16])
        total = dr_buf[0].astype(F32)
        for i in range(1, 16):
            total = total + dr_buf[i].astype(F32)
        e_buf[d, t] = (total * GRAD_SCALE).astype(BF16)
        for i in range(1, 16):
            piece_keys[i] = send(e_buf.at[d, t], e_buf.at[d, t], (d, (t + i) % 16))[0]

    z_keys, down_keys, piece_keys = {}, {}, {}
    e_gather = ZGather(
        lambda u, core: e_buf.at[2 * u + core],
        lambda u, core, i: e_buf.at[2 * u + core, pl.ds(8 * i, 8)],
    )

    d_gather.have(0)
    gradients(0)
    product2(0, rank_terms(0))
    d_gather.onward()
    advance(0)
    d_gather.have(3)
    gradients(3)
    product2(3, rank_terms(3))
    d_gather.last()
    advance(1)
    d_gather.have(1)
    gradients(1)
    product2(1, rank_terms(1))
    advance(2)
    d_gather.have(2)
    ab_gather.have(2)
    gradients(2)
    ranks = rank_terms(2)
    for i in range(1, 16):
        to = (t + i) % 16
        z_keys[i] = send(zs.at[to], zr.at[t], (d, to))[0]
    product2(2, ranks)
    advance(3)
    z_sum()
    advance(4)
    down_sum()
    advance(5)
    for i in range(1, 16):
        whose = (t + 16 - i) % 16
        arrived(piece_keys[i], e_buf.at[d, whose])
    e_gather.begin()
    advance(6)

    grads_up = [jnp.zeros((2 * RANK, HID), F32), jnp.zeros((2 * RANK, HID), F32)]
    for u in range(4):
        low = adn[:, u].astype(F32)
        rows = jnp.concatenate([low[:, :8].reshape(128, HB), low[:, 8:].reshape(128, HB)], axis=0)
        turned = jnp.transpose(rows)[: 2 * RANK].astype(BF16)
        for i in range(2):
            grads_up[i] = grads_up[i] + jnp.dot(turned, ab[u, i].reshape(256, HID), preferred_element_type=F32)
    up_ref[0] = grads_up[0][:RANK] * GRAD_SCALE
    up_ref[1] = grads_up[1][RANK:] * GRAD_SCALE

    e_gather.onward()
    advance(7)
    e_gather.last()
    for k, o in rels:
        arrived(last_a2a[k, o], v_buf.at[source(k, o)])
    for p in range(8):
        value = v_buf[p]
        out_ref[0, :, p * SLICE : p * SLICE + HALF] = value[:8]
        out_ref[0, :, p * SLICE + HALF : (p + 1) * SLICE] = value[8:]
    for rel in range(4):
        e_gather.have(rel)
    for p in range(8):
        for i in range(16):
            start = p * SLICE + HB * i
            down_ref[:, start : start + HB] = e_buf[p, i].astype(F32)
    for copy in pending:
        copy.wait_send()
    assert count[0] == NSEM


def on_device(kept, grad, gate_pre, up_pre, wg, wu, wd, a_maps, u_maps):
    vmem = pl.BlockSpec(memory_space=pltpu.VMEM)
    hbm = pl.BlockSpec(memory_space=pl.ANY)
    shapes = [
        (HID, SLICE), (SLICE, HID), (SLICE, HID),
        (2, 8, 16, HALF), (2, 8, 16, HALF),
        (4, 4, 4, 16, SLICE),
        (4, 16, SLICE),
        (4, 2, 128, HID), (4, 128, HID), (2, 64, HID), (2, 128, HID), (4, 2, 128, HID),
        (4, 2, 2, 128, HID),
        (4, 4, 4, 16, SLICE),
        (4, 2, 2, 2, 16, HALF), (4, 2, 2, 4, 16, HALF), (4, 2, 2, 16, 512), (4, 2, 2, 16, HALF),
        (8, 16, HALF), (8, 16, HALF),
        (16, HB), (8, 16, HB), (16, 4, 16, HB),
        (16, 4, 16, HB), (16, 4, 16, HB),
        (16, 2 * RANK, HB), (16, 2 * RANK, HB), (8, 16, 2 * RANK, HB),
        (2 * RANK, SLICE), (2, 2 * RANK, HID),
    ]
    out, down, up = pl.pallas_call(
        kernel,
        out_shape=(
            jax.ShapeDtypeStruct((1, 8, WIDTH), BF16),
            jax.ShapeDtypeStruct((2 * RANK, WIDTH), F32),
            jax.ShapeDtypeStruct((2, RANK, HID), F32),
        ),
        in_specs=[vmem] * 7 + [hbm] * 3,
        out_specs=(vmem,) * 3,
        scratch_shapes=[pltpu.VMEM(s, BF16) for s in shapes]
        + [
            pltpu.SemaphoreType.DMA((NSEM,)),
            pltpu.SemaphoreType.DMA((NSEM,)),
            pltpu.SemaphoreType.DMA((3,)),
        ],
        compiler_params=pltpu.CompilerParams(
            collective_id=0, has_side_effects=True, vmem_limit_bytes=66_000_000
        ),
        name="gated_backward",
    )(kept, grad, gate_pre, up_pre, a_maps, u_maps, jnp.asarray(sign_table(), BF16), wd, wg, wu)
    return out, down.reshape(2, RANK, WIDTH), up


def solution(mesh):
    placed = (
        P("dp", "tensor", None),
        P("dp", "tensor", None),
        P("dp", None, "tensor"),
        P("dp", None, "tensor"),
        P("dp", "tensor"),
        P("dp", "tensor"),
        P("tensor", "dp"),
        P(),
        P(None, None, "tensor"),
    )
    return jax.shard_map(
        on_device,
        mesh=mesh,
        in_specs=placed,
        out_specs=(P("dp", "tensor", None), P(), P(None, None, "tensor")),
        check_vma=False,
    )
```

time: 739 us -> 137 us (0.19)
  waiting for transfers between devices: 484 us -> 0 us
  Pallas kernels: 0 us -> 130 us
  other arithmetic: 98.6 us -> 0 us
  matrix products: 51.4 us -> 0 us
  local copies, waits for them, and re-layouts: 50.9 us -> 6.34 us
  blocking collectives: 32.1 us -> 0 us
  between operations: 14.9 us -> 0.64 us
    psum x2 -> x0, waiting for transfers between devices: 206 us -> none  [the longest x1 149 us: on_device(): down_map_total = lax.psum(down_map_terms, ('dp', 'tensor'))]
    pallas_call x0 -> x1, Pallas kernels: none -> 130 us  [on_device(): pl.pallas_call(kernel, out_shape=(jax.ShapeDtypeStruct((1, 8, WIDTH), BF1...]
    unnamed x9 -> x0, waiting for transfers between devices: 105 us -> none
    unnamed x1 -> x0, other arithmetic: 90.8 us -> none
    all_gather x3 -> x0, waiting for transfers between devices: 86.3 us -> none  [the longest x1 51.3 us: on_device(): lax.all_gather(grad_split, 'tensor', axis=1, tiled=True)]
    reduce_scatter x2 -> x0, waiting for transfers between devices: 86.3 us -> none  [the longest x1 44.3 us: on_device(): lax.psum_scatter(hidden_part, 'dp', scatter_dimension=0, tiled=True)]
    dot_general x12 -> x0, matrix products: 51.4 us -> none  [the longest x5 40.3 us: contract_trailing(): lax.dot_general(left, right, (((2,), (1,)), ((), ())), preferred_element_...]
    all_gather x1 -> x0, blocking collectives: 19 us -> none  [on_device(): lax.all_gather(adapter_own, 'tensor', axis=1, tiled=True)]
  transfers between devices with their start and end apart: 9 -> 0, of which waited for: 8 -> 0; matrix products, arithmetic and copies ran while one was open for 6% -> 0% of each run, Pallas kernels for 0% -> 0%
where the time goes in v1:
time: 137 us
  Pallas kernels  130 us (95%)
  local copies, waits for them, and re-layouts  6.34 us (5%)
    pallas_call x1, Pallas kernels, on_device(): pl.pallas_call(kernel, out_shape=(jax.ShapeDtypeStruct((1, 8, WIDTH), BF1...  130 us
    unnamed x3, local copies, waits for them, and re-layouts  6.34 us

profile of v1, /device:TPU:1, one launch (start us, length us, event | category | flops | bytes accessed | tf_op | source)
XLA Modules:
  0.0 136.7 jit_solution(7816135506198799705)
XLA Ops:
  0.6 129.7 %gated_backward.1 = (bf16[1,8,16384]{2,1,0:T(8,128)(2,1)}, f32[32,16384]{1,0:T(8,128)}, f32[2,16,1664]{2,1,0:T(8,128)}) custom-call(bf16[1,8,16384]{2,1,0:T(8,128)(2,1)} %x_ref.1, bf16[1,8,16384]{2,1,0:T(8,128)(2,1)} %dy_ref.1, bf16[1,128,1664]{2,1,0:T(8,128)(2,1)} %g_ref.1, bf16[1,128,1664]{2,1,0:T(8,128)(2,1)} %u_ref.1, bf16[2,16,16384]{2,1,0:T(8,128)(2,1)} %am_ref.1, ...), custom_call_target="tpu_custom_call" | custom-call | tf_op jit(solution)/shard_map/gated_backward/pallas_call | solution.py:647
  130.4 1.7 %copy.16 = bf16[1,8,16384]{2,1,0:T(8,128)(2,1)} copy(bf16[1,8,16384]{2,1,0:T(8,128)(2,1)} %get-tuple-element.12) | data formatting | bytes 524288
  132.0 3.0 %copy.17 = f32[2,16,16384]{2,1,0:T(8,128)} copy(f32[2,16,16384]{2,1,0:T(8,128)} %bitcast.1) | data formatting | bytes 4194304
  135.1 1.6 %copy.18 = f32[2,16,1664]{2,1,0:T(8,128)} copy(f32[2,16,1664]{2,1,0:T(8,128)} %get-tuple-element.14) | data formatting | bytes 425984

commit v2 on v1

--- a/solution.py
+++ b/solution.py
@@ -22,7 +22,7 @@
 ORDER2 = (0, 3, 1, 2)
 TILES1 = ((0, 640), (640, 512), (1152, 512))
 TILE2 = 512
-NSEM = 264
+NSEM = 301
 NT = (((1,), (1,)), ((), ()))
 
 
@@ -36,9 +36,9 @@
 
 
 def kernel(
-    x_ref, dy_ref, g_ref, u_ref, am_ref, um_ref, h_ref, wd_hbm, wg_hbm, wu_hbm,
-    out_ref, down_ref, up_ref,
-    wd, wg, wu, s_buf, r_buf, y_buf, xg, p_buf, q_buf, f_buf, gz_buf, d_buf, ab, o_buf,
+    x_hbm, dy_hbm, g_hbm, u_hbm, am_hbm, um_hbm, h_hbm, wd_hbm, wg_hbm, wu_hbm,
+    v_hbm, e_hbm, up_hbm,
+    x_ref, dy_ref, g_ref, u_ref, am_ref, um_ref, h_ref, up_ref, wd, wg, wu, s_buf, r_buf, y_buf, xg, p_buf, q_buf, f_buf, gz_buf, d_buf, ab, o_buf,
     r1, r2, r3, r4, t_buf, v_buf, ad_s, ad_r, adn, zs, zr, ds_buf, dr_buf, e_buf, a_own, u_pad,
     ss, rs, ws,
 ):
@@ -83,11 +83,18 @@
         copy.wait_send()
         pending[:] = [other for other in pending if other is not copy]
 
-    loads = []
-    for k, (src, dst) in enumerate(((wd_hbm, wd), (wg_hbm, wg), (wu_hbm, wu))):
-        copy = pltpu.make_async_copy(src, dst, ws.at[k])
-        copy.start()
-        loads.append(copy)
+    loads = {}
+    for k, (name, src, dst) in enumerate((
+        ("h", h_hbm, h_ref), ("g", g_hbm, g_ref), ("u", u_hbm, u_ref), ("dy", dy_hbm, dy_ref), ("x", x_hbm, x_ref),
+        ("am", am_hbm, am_ref), ("um", um_hbm, um_ref), ("wd", wd_hbm, wd), ("wg", wg_hbm, wg), ("wu", wu_hbm, wu),
+    )):
+        loads[name] = pltpu.make_async_copy(src, dst, ws.at[k])
+        if k < 7:
+            loads[name].start()
+
+    def loaded(*names):
+        for name in names:
+            loads[name].wait()
 
     barrier = pltpu.get_barrier_semaphore()
     for i in range(1, 8):
@@ -114,18 +121,6 @@
     def source(k, o):
         return unit((4 - k) % 4) * 2 + (oc if o else c)
 
-    rotate(dy_ref, 0)
-    pl.semaphore_wait(barrier, 22)
-    first_a2a = {}
-    for slot in range(2):
-        if slot == 1:
-            rotate(x_ref, 1)
-        for k, o in rels:
-            first_a2a[slot, k, o] = send(
-                s_buf.at[slot, peer(k, o)], r_buf.at[slot, d], (peer(k, o), t)
-            )[0]
-        r_buf[slot, d] = s_buf[slot, d]
-
     def factors(i, carry):
         rows = pl.ds(pl.multiple_of(i * 16, 16), 16)
         gate = g_ref[0, rows, :].astype(F32)
@@ -135,7 +130,21 @@
         ab[z, 1, c, rows, :] = (gate * squash).astype(BF16)
         return carry
 
+    first_a2a = {}
+
+    def exchange(slot):
+        for k, o in rels:
+            first_a2a[slot, k, o] = send(
+                s_buf.at[slot, peer(k, o)], r_buf.at[slot, d], (peer(k, o), t)
+            )[0]
+        r_buf[slot, d] = s_buf[slot, d]
+
+    loaded("g", "u")
     lax.fori_loop(0, 8, factors, 0)
+    loaded("h", "dy")
+    rotate(dy_ref, 0)
+    pl.semaphore_wait(barrier, 22)
+    exchange(0)
 
     class ZGather:
         def __init__(self, whole, half):
@@ -153,13 +162,17 @@
             self.copies[owner].append(copy)
             return k
 
-        def onward(self):
+        def across(self):
             arrived(self.k_up, self.whole(zm, c))
-            self.k_f0 = self.push(3, self.half(zm, c, 0), up_dev)
             self.k_from[3] = self.push(3, self.whole(zm, c), sib)
             arrived(self.k_down, self.whole(zp, c))
+            self.k_from[1] = self.push(1, self.whole(zp, c), sib)
+
+        def pass_up(self):
+            self.k_f0 = self.push(3, self.half(zm, c, 0), up_dev)
+
+        def pass_down(self):
             self.k_f1 = self.push(1, self.half(zp, c, 1), down_dev)
-            self.k_from[1] = self.push(1, self.whole(zp, c), sib)
 
         def last(self):
             arrived(self.k_f0, self.half(unit(2), c, 0))
@@ -172,12 +185,16 @@
         def release(self, rel):
             for copy in self.copies[rel]:
                 sent(copy)
+            self.copies[rel] = []
 
     ab_gather = ZGather(
         lambda u, core: ab.at[u, :, core],
         lambda u, core, i: ab.at[u, i, core],
     )
     ab_gather.begin()
+    loaded("x")
+    rotate(x_ref, 1)
+    exchange(1)
 
     def unpack(slot, u):
         low = r_buf[slot, 2 * u].astype(F32)
@@ -200,25 +217,25 @@
         return buf.at[lead, yy, xx, :, cols]
 
     COLS = (pl.ds(0, HALF), pl.ds(HALF, HALF))
-    chunks = ((0, 2), (2, 2))
+    chunks = ((0, 1), (1, 2), (3, 1))
     keys = {}
 
     def shift(axis, k):
         return (pos[axis] + k) % 4
 
-    def lead_of(n, part):
-        start, size = chunks[n]
-        if part == "all":
-            return pl.ds(start, size)
-        return pl.ds(start, size // 2) if part == "first" else pl.ds(start + size // 2, size // 2)
+    def half_cols(h, i):
+        return pl.ds(HALF * h + 512 * i, 512)
+
+    def cols_of(h, part):
+        return COLS[h] if part == "all" else half_cols(h, 0 if part == "first" else 1)
 
     def ag1_ref(n, h, fr, part):
         f_axis, g_axis = AXES[h]
-        return block(y_buf, lead_of(n, part), h, shift(f_axis, fr), pos[g_axis], COLS[h])
+        return block(y_buf, pl.ds(*chunks[n]), h, shift(f_axis, fr), pos[g_axis], cols_of(h, part))
 
     def ag2_ref(n, h, fr, gr, part):
         f_axis, g_axis = AXES[h]
-        return block(y_buf, lead_of(n, part), h, shift(f_axis, fr), shift(g_axis, gr), COLS[h])
+        return block(y_buf, pl.ds(*chunks[n]), h, shift(f_axis, fr), shift(g_axis, gr), cols_of(h, part))
 
     def ag_push(key, ref, axis, k):
         keys[key] = send(ref, ref, near(axis, k))[0]
@@ -270,7 +287,15 @@
                     arrived(keys["2f", n, h, fr, k], ag2_ref(n, h, fr, 2, part))
 
     ag_step0(0)
+    loads["wd"].start()
+    ag_step1(0)
     ag_step0(1)
+    ag_step2(0)
+    ag_step3(0)
+    ag_step1(1)
+    ag_step4(0)
+    ag_step2(1)
+    loaded("am", "um", "wd")
 
     a_own[...] = am_ref[:, :, pl.ds(pl.multiple_of(d * SLICE, SLICE), SLICE)].reshape(2 * RANK, SLICE)
     u_pad[0, :RANK] = um_ref[0]
@@ -279,53 +304,45 @@
     u_pad[1, :RANK] = jnp.zeros((RANK, HID), BF16)
     zs[...] = jnp.zeros_like(zs)
     ad_s[...] = jnp.zeros_like(ad_s)
-    tops = jnp.zeros((16, 2 * RANK), F32)
-    bottoms = jnp.zeros((16, 2 * RANK), F32)
-    for p in range(8):
-        tokens = s_buf[1, p]
-        for part in range(2):
-            start = p * SLICE + part * HALF
-            maps = am_ref[:, :, start : start + HALF].reshape(2 * RANK, HALF)
-            value = lax.dot_general(tokens, maps, NT, preferred_element_type=F32)
-            if part == 0:
-                tops = tops + value
-            else:
-                bottoms = bottoms + value
-    ad_s[:, : 2 * RANK] = jnp.concatenate([tops[:8] + bottoms[8:], jnp.zeros((8, 2 * RANK), F32)], axis=0).astype(BF16)
-
-    ag_step1(0)
-    ag_step1(1)
-
-    ad_keys = {}
-    for k, o in rels:
-        ad_keys[k, o] = send(ad_s, ad_r.at[d], (peer(k, o), t))[0]
-    ad_r[d] = ad_s[...]
-    for k, o in rels:
-        arrived(first_a2a[1, k, o], r_buf.at[1, source(k, o)])
-    for u in range(4):
-        left, right = unpack(1, u)
-        xg[u, :, :HALF] = left
-        xg[u, :, HALF:] = right
-
-    ag_step2(0)
-    ag_step2(1)
-    for k, o in rels:
-        arrived(ad_keys[k, o], ad_r.at[source(k, o)])
-    for u in range(4):
-        adn[t, u] = jnp.concatenate(
-            [ad_r[2 * u].astype(F32)[:8], ad_r[2 * u + 1].astype(F32)[:8]], axis=0
-        ).astype(BF16)
-    adt_keys = {}
-    for i in range(1, 16):
-        adt_keys[i] = send(adn.at[t], adn.at[t], (d, (t + i) % 16))[0]
-    ag_step3(0)
-    ag_step3(1)
-    ab_gather.onward()
-    ag_step4(0)
-    ag_step4(1)
-
-    loads[0].wait()
-    core_keys = {}
+    def adapter_down():
+        tops = jnp.zeros((16, 2 * RANK), F32)
+        bottoms = jnp.zeros((16, 2 * RANK), F32)
+        for p in range(8):
+            tokens = s_buf[1, p]
+            for part in range(2):
+                start = p * SLICE + part * HALF
+                maps = am_ref[:, :, start : start + HALF].reshape(2 * RANK, HALF)
+                value = lax.dot_general(tokens, maps, NT, preferred_element_type=F32)
+                if part == 0:
+                    tops = tops + value
+                else:
+                    bottoms = bottoms + value
+        ad_s[:, : 2 * RANK] = jnp.concatenate([tops[:8] + bottoms[8:], jnp.zeros((8, 2 * RANK), F32)], axis=0).astype(BF16)
+
+    def adapters_out():
+        for k, o in rels:
+            ad_keys[k, o] = send(ad_s, ad_r.at[d], (peer(k, o), t))[0]
+        ad_r[d] = ad_s[...]
+
+    def adapters_on():
+        for k, o in rels:
+            arrived(ad_keys[k, o], ad_r.at[source(k, o)])
+        for u in range(4):
+            adn[t, u] = jnp.concatenate(
+                [ad_r[2 * u].astype(F32)[:8], ad_r[2 * u + 1].astype(F32)[:8]], axis=0
+            ).astype(BF16)
+        for i in range(1, 16):
+            adt_keys[i] = send(adn.at[t], adn.at[t], (d, (t + i) % 16))[0]
+
+    def inputs_in():
+        for k, o in rels:
+            arrived(first_a2a[1, k, o], r_buf.at[1, source(k, o)])
+        for u in range(4):
+            left, right = unpack(1, u)
+            xg[u, :, :HALF] = left
+            xg[u, :, HALF:] = right
+
+    ad_keys, adt_keys, core_keys = {}, {}, {}
 
     def product1(i):
         rows = y_buf[i].reshape(256, SLICE)
@@ -350,15 +367,26 @@
 
         lax.fori_loop(0, (hi - lo) // 16, body, 0)
 
+    own = [p_buf.at[i, c] for i in range(4)]
     ag_step5(0)
     product1(0)
-    product1(1)
-    ag_step5(1)
-    own = [p_buf.at[i, c] for i in range(4)]
+    ag_step0(2)
+    loads["wg"].start()
+    ag_step3(1)
+    ag_step1(2)
     arrived(core_keys[0], q_buf.at[0])
     add_rows((own[0], own[0]), [(q_buf.at[0], 0)])
     k_f0 = send(p_buf.at[0, c, pl.ds(0, 64)], f_buf.at[0], up_dev)[0]
     k_f1 = send(p_buf.at[0, c, pl.ds(64, 64)], f_buf.at[1], down_dev)[0]
+    ag_step4(1)
+    ag_step2(2)
+    adapter_down()
+    adapters_out()
+    ag_step3(2)
+    loads["wu"].start()
+    ag_step5(1)
+    product1(1)
+    ag_step4(2)
     product1(2)
     arrived(core_keys[1], q_buf.at[1])
     arrived(k_f0, f_buf.at[0])
@@ -370,31 +398,31 @@
     add_rows((own[2], own[2]), [(q_buf.at[2], 0)], 0, 64)
     add_rows((own[2], own[2]), [(q_buf.at[2], 0), (f_buf.at[1], 64)], 64, 128)
     k_g1 = send(p_buf.at[2, c], gz_buf.at[1], down_dev)[0]
+    ag_step5(2)
     product1(3)
-    ab_gather.last()
-    ab_gather.have(0)
-    ab_gather.have(3)
-    ab_gather.have(1)
-    for i in range(1, 16):
-        arrived(adt_keys[i], adn.at[(t + 16 - i) % 16])
+    adapters_on()
+    inputs_in()
+    loaded("wg", "wu")
     arrived(core_keys[3], q_buf.at[3])
+    add_rows((own[3], own[3]), [(q_buf.at[3], 0)])
+    ab_gather.across()
+    for rel in (0, 3, 1):
+        ab_gather.have(rel)
+        ab_gather.release(rel)
     arrived(k_g0, gz_buf.at[0])
     arrived(k_g1, gz_buf.at[1])
-    add_rows((own[3], d_buf.at[z, c]), [(q_buf.at[3], 0), (gz_buf.at[0], 0), (gz_buf.at[1], 0)])
+    add_rows((own[3], d_buf.at[z, c]), [(gz_buf.at[0], 0), (gz_buf.at[1], 0)])
 
     d_gather = ZGather(
         lambda u, core: d_buf.at[u, core],
-        lambda u, core, i: d_buf.at[u, core, pl.ds(64 * i, 64)],
+        None,
     )
     d_gather.begin()
-    loads[1].wait()
-    loads[2].wait()
 
     rs_keys = {}
 
     def gradients(rel):
         u = unit(rel)
-        ab_gather.release(rel)
         for core in range(2):
 
             def body(i, carry):
@@ -422,18 +450,18 @@
         zs[:, u, :, : 2 * RANK] = by_token(ranks).astype(BF16).reshape(16, 16, 2 * RANK)
         return (SCALE * ranks).astype(BF16)
 
-    def product2(rel, ranks):
+    def product2(rel, ranks, h):
         u = unit(rel)
 
         def body(n, carry):
-            rows = pl.ds(pl.multiple_of(n * TILE2, TILE2), TILE2)
+            rows = pl.ds(pl.multiple_of(HALF * h + n * TILE2, TILE2), TILE2)
             value = lax.dot_general(ab[u, 0].reshape(256, HID), wg[rows, :], NT, preferred_element_type=F32)
             value = value + lax.dot_general(ab[u, 1].reshape(256, HID), wu[rows, :], NT, preferred_element_type=F32)
             value = value + jnp.dot(ranks, a_own[:, rows], preferred_element_type=F32)
             o_buf[u, :, :, :, rows] = by_token(value).astype(BF16).reshape(4, 4, 16, TILE2)
             return carry
 
-        lax.fori_loop(0, SLICE // TILE2, body, 0)
+        lax.fori_loop(0, HALF // TILE2, body, 0)
 
     RAXES = (("y", "x"), ("x", "y"))
 
@@ -444,68 +472,63 @@
     def add_into(dst, src):
         dst[...] = (dst[...].astype(F32) + src[...].astype(F32)).astype(BF16)
 
-    def rs_step1(rel):
-        u = unit(rel)
-        for h in (0, 1):
-            f_axis = RAXES[h][0]
-            for i, k in enumerate((1, -1)):
-                rs_keys["1", rel, h, k] = send(
-                    out_block(u, h, shift(f_axis, 2), pl.ds(2 * i, 2), COLS[h]),
-                    r1.at[u, h, i],
-                    near(f_axis, k),
-                )[0]
-
-    def rs_step2(rel):
-        u = unit(rel)
-        for h in (0, 1):
-            f_axis = RAXES[h][0]
-            for i, k in enumerate((1, -1)):
-                arrived(rs_keys["1", rel, h, k], r1.at[u, h, i])
-                for j in range(2):
-                    add_into(out_block(u, h, shift(f_axis, k), 2 * i + j, COLS[h]), r1.at[u, h, i, j])
-                rs_keys["2", rel, h, k] = send(
-                    out_block(u, h, shift(f_axis, k), pl.ds(0, 4), COLS[h]),
-                    r2.at[u, h, i],
-                    near(f_axis, k),
-                )[0]
-
-    def half_cols(h, i):
-        return pl.ds(HALF * h + 512 * i, 512)
-
-    def rs_step3(rel):
-        u = unit(rel)
-        for h in (0, 1):
-            f_axis, g_axis = RAXES[h]
-            for i, k in enumerate((1, -1)):
-                arrived(rs_keys["2", rel, h, k], r2.at[u, h, i])
-            for j in range(4):
-                dst = out_block(u, h, pos[f_axis], j, COLS[h])
-                dst[...] = (
-                    dst[...].astype(F32) + r2[u, h, 0, j].astype(F32) + r2[u, h, 1, j].astype(F32)
-                ).astype(BF16)
-            for i, k in enumerate((1, -1)):
-                rs_keys["3", rel, h, k] = send(
-                    out_block(u, h, pos[f_axis], shift(g_axis, 2), half_cols(h, i)),
-                    r3.at[u, h, i],
-                    near(g_axis, k),
-                )[0]
-
-    def rs_step4(rel):
-        u = unit(rel)
-        for h in (0, 1):
-            f_axis, g_axis = RAXES[h]
-            for i, k in enumerate((1, -1)):
-                arrived(rs_keys["3", rel, h, k], r3.at[u, h, i])
-                add_into(out_block(u, h, pos[f_axis], shift(g_axis, k), half_cols(h, i)), r3.at[u, h, i])
-                rs_keys["4", rel, h, k] = send(
-                    out_block(u, h, pos[f_axis], shift(g_axis, k), COLS[h]),
-                    r4.at[u, h, i],
-                    near(g_axis, k),
-                )[0]
+    def rs_step1(rel, h):
+        u = unit(rel)
+        f_axis = RAXES[h][0]
+        for i, k in enumerate((1, -1)):
+            rs_keys["1", rel, h, k] = send(
+                out_block(u, h, shift(f_axis, 2), pl.ds(2 * i, 2), COLS[h]),
+                r1.at[u, h, i],
+                near(f_axis, k),
+            )[0]
+
+    def rs_step2(rel, h):
+        u = unit(rel)
+        f_axis = RAXES[h][0]
+        for i, k in enumerate((1, -1)):
+            arrived(rs_keys["1", rel, h, k], r1.at[u, h, i])
+            for j in range(2):
+                add_into(out_block(u, h, shift(f_axis, k), 2 * i + j, COLS[h]), r1.at[u, h, i, j])
+            rs_keys["2", rel, h, k] = send(
+                out_block(u, h, shift(f_axis, k), pl.ds(0, 4), COLS[h]),
+                r2.at[u, h, i],
+                near(f_axis, k),
+            )[0]
+
+    def rs_step3(rel, h):
+        u = unit(rel)
+        f_axis, g_axis = RAXES[h]
+        for i, k in enumerate((1, -1)):
+            arrived(rs_keys["2", rel, h, k], r2.at[u, h, i])
+        for j in range(4):
+            dst = out_block(u, h, pos[f_axis], j, COLS[h])
+            dst[...] = (
+                dst[...].astype(F32) + r2[u, h, 0, j].astype(F32) + r2[u, h, 1, j].astype(F32)
+            ).astype(BF16)
+        for i, k in enumerate((1, -1)):
+            rs_keys["3", rel, h, k] = send(
+                out_block(u, h, pos[f_axis], shift(g_axis, 2), half_cols(h, i)),
+                r3.at[u, h, i],
+                near(g_axis, k),
+            )[0]
+
+    def rs_step4(rel, h):
+        u = unit(rel)
+        f_axis, g_axis = RAXES[h]
+        for i, k in enumerate((1, -1)):
+            arrived(rs_keys["3", rel, h, k], r3.at[u, h, i])
+            add_into(out_block(u, h, pos[f_axis], shift(g_axis, k), half_cols(h, i)), r3.at[u, h, i])
+            rs_keys["4", rel, h, k] = send(
+                out_block(u, h, pos[f_axis], shift(g_axis, k), COLS[h]),
+                r4.at[u, h, i],
+                near(g_axis, k),
+            )[0]
 
     last_a2a = {}
 
-    def rs_step5(rel):
+    def rs_step5(rel, h):
+        if h == 0:
+            return
         u = unit(rel)
         halves = []
         for h in (0, 1):
@@ -525,11 +548,12 @@
 
     steps = (rs_step1, rs_step2, rs_step3, rs_step4, rs_step5)
 
+    items = [(rel, h) for rel in ORDER2 for h in (0, 1)]
+
     def advance(turn):
-        for s in range(5):
-            i = turn - s
-            if 0 <= i < 4:
-                steps[s](ORDER2[i])
+        for k in range(5):
+            if 0 <= turn - k < 8:
+                steps[k](*items[turn - k])
 
     def z_sum():
         for i in range(1, 16):
@@ -563,72 +587,105 @@
         lambda u, core, i: e_buf.at[2 * u + core, pl.ds(8 * i, 8)],
     )
 
-    d_gather.have(0)
-    gradients(0)
-    product2(0, rank_terms(0))
-    d_gather.onward()
-    advance(0)
-    d_gather.have(3)
-    gradients(3)
-    product2(3, rank_terms(3))
-    d_gather.last()
-    advance(1)
-    d_gather.have(1)
-    gradients(1)
-    product2(1, rank_terms(1))
-    advance(2)
-    d_gather.have(2)
-    ab_gather.have(2)
-    gradients(2)
-    ranks = rank_terms(2)
-    for i in range(1, 16):
-        to = (t + i) % 16
-        z_keys[i] = send(zs.at[to], zr.at[t], (d, to))[0]
-    product2(2, ranks)
-    advance(3)
-    z_sum()
-    advance(4)
-    down_sum()
-    advance(5)
-    for i in range(1, 16):
-        whose = (t + 16 - i) % 16
-        arrived(piece_keys[i], e_buf.at[d, whose])
-    e_gather.begin()
-    advance(6)
-
     grads_up = [jnp.zeros((2 * RANK, HID), F32), jnp.zeros((2 * RANK, HID), F32)]
-    for u in range(4):
+
+    def up_grads(rel):
+        u = unit(rel)
         low = adn[:, u].astype(F32)
         rows = jnp.concatenate([low[:, :8].reshape(128, HB), low[:, 8:].reshape(128, HB)], axis=0)
         turned = jnp.transpose(rows)[: 2 * RANK].astype(BF16)
         for i in range(2):
             grads_up[i] = grads_up[i] + jnp.dot(turned, ab[u, i].reshape(256, HID), preferred_element_type=F32)
+
+    d_gather.have(0)
+    gradients(0)
+    ranks = rank_terms(0)
+    product2(0, ranks, 0)
+    advance(0)
+    product2(0, ranks, 1)
+    advance(1)
+    d_gather.across()
+    d_gather.have(3)
+    gradients(3)
+    ab_gather.pass_up()
+    d_gather.have(1)
+    gradients(1)
+    ab_gather.pass_down()
+    ranks = rank_terms(3)
+    product2(3, ranks, 0)
+    advance(2)
+    product2(3, ranks, 1)
+    advance(3)
+    ranks = rank_terms(1)
+    product2(1, ranks, 0)
+    advance(4)
+    product2(1, ranks, 1)
+    ab_gather.last()
+    advance(5)
+    ab_gather.have(2)
+    ranks = rank_terms(2)
+    for i in range(1, 16):
+        to = (t + i) % 16
+        z_keys[i] = send(zs.at[to], zr.at[t], (d, to))[0]
+    product2(2, ranks, 0)
+    advance(6)
+    z_sum()
+    product2(2, ranks, 1)
+    advance(7)
+    down_sum()
+    for i in range(1, 16):
+        arrived(adt_keys[i], adn.at[(t + 16 - i) % 16])
+    up_grads(0)
+    up_grads(3)
+    advance(8)
+    for i in range(1, 16):
+        arrived(piece_keys[i], e_buf.at[d, (t + 16 - i) % 16])
+    e_gather.begin()
+    advance(9)
+    up_grads(1)
+    up_grads(2)
     up_ref[0] = grads_up[0][:RANK] * GRAD_SCALE
     up_ref[1] = grads_up[1][RANK:] * GRAD_SCALE
-
-    e_gather.onward()
-    advance(7)
+    stores = [pltpu.make_async_copy(up_ref, up_hbm, ws.at[0])]
+    stores[0].start()
+    advance(10)
+    e_gather.across()
+    e_gather.pass_up()
+    e_gather.pass_down()
+    advance(11)
     e_gather.last()
+    for rel in range(4):
+        e_gather.have(rel)
+    stores.append(pltpu.make_async_copy(e_buf, e_hbm, ws.at[1]))
+    stores[1].start()
     for k, o in rels:
         arrived(last_a2a[k, o], v_buf.at[source(k, o)])
+    stores.append(pltpu.make_async_copy(v_buf, v_hbm, ws.at[2]))
+    stores[2].start()
+    for copy in pending:
+        copy.wait_send()
+    for copy in stores:
+        copy.wait()
+    assert count[0] == NSEM
+
+
+def finish(v_ref, e_ref, up_in, out_ref, down_ref, up_ref):
     for p in range(8):
-        value = v_buf[p]
+        value = v_ref[p]
         out_ref[0, :, p * SLICE : p * SLICE + HALF] = value[:8]
         out_ref[0, :, p * SLICE + HALF : (p + 1) * SLICE] = value[8:]
-    for rel in range(4):
-        e_gather.have(rel)
-    for p in range(8):
         for i in range(16):
             start = p * SLICE + HB * i
-            down_ref[:, start : start + HB] = e_buf[p, i].astype(F32)
-    for copy in pending:
-        copy.wait_send()
-    assert count[0] == NSEM
+            down_ref[:, start : start + HB] = e_ref[p, i].astype(F32)
+    up_ref[...] = up_in[...]
 
 
 def on_device(kept, grad, gate_pre, up_pre, wg, wu, wd, a_maps, u_maps):
     vmem = pl.BlockSpec(memory_space=pltpu.VMEM)
     hbm = pl.BlockSpec(memory_space=pl.ANY)
+    operands = [
+        (1, 8, WIDTH), (1, 8, WIDTH), (1, 128, HID), (1, 128, HID), (2, RANK, WIDTH), (2, RANK, HID), (HB, HB),
+    ]
     shapes = [
         (HID, SLICE), (SLICE, HID), (SLICE, HID),
         (2, 8, 16, HALF), (2, 8, 16, HALF),
@@ -644,26 +701,39 @@
         (16, 2 * RANK, HB), (16, 2 * RANK, HB), (8, 16, 2 * RANK, HB),
         (2 * RANK, SLICE), (2, 2 * RANK, HID),
     ]
-    out, down, up = pl.pallas_call(
+    results = pl.pallas_call(
         kernel,
         out_shape=(
-            jax.ShapeDtypeStruct((1, 8, WIDTH), BF16),
-            jax.ShapeDtypeStruct((2 * RANK, WIDTH), F32),
+            jax.ShapeDtypeStruct((8, 16, HALF), BF16),
+            jax.ShapeDtypeStruct((8, 16, 2 * RANK, HB), BF16),
             jax.ShapeDtypeStruct((2, RANK, HID), F32),
         ),
-        in_specs=[vmem] * 7 + [hbm] * 3,
-        out_specs=(vmem,) * 3,
-        scratch_shapes=[pltpu.VMEM(s, BF16) for s in shapes]
+        in_specs=[hbm] * 10,
+        out_specs=(hbm,) * 3,
+        scratch_shapes=[pltpu.VMEM(s, BF16) for s in operands]
+        + [pltpu.VMEM((2, RANK, HID), F32)]
+        + [pltpu.VMEM(s, BF16) for s in shapes]
         + [
             pltpu.SemaphoreType.DMA((NSEM,)),
             pltpu.SemaphoreType.DMA((NSEM,)),
-            pltpu.SemaphoreType.DMA((3,)),
+            pltpu.SemaphoreType.DMA((10,)),
         ],
         compiler_params=pltpu.CompilerParams(
             collective_id=0, has_side_effects=True, vmem_limit_bytes=66_000_000
         ),
         name="gated_backward",
     )(kept, grad, gate_pre, up_pre, a_maps, u_maps, jnp.asarray(sign_table(), BF16), wd, wg, wu)
+    out, down, up = pl.pallas_call(
+        finish,
+        out_shape=(
+            jax.ShapeDtypeStruct((1, 8, WIDTH), BF16),
+            jax.ShapeDtypeStruct((2 * RANK, WIDTH), F32),
+            jax.ShapeDtypeStruct((2, RANK, HID), F32),
+        ),
+        in_specs=[vmem] * 3,
+        out_specs=(vmem,) * 3,
+        name="finish",
+    )(*results)
     return out, down.reshape(2, RANK, WIDTH), up
 
 

time: 137 us -> 129 us (0.942)
  local copies, waits for them, and re-layouts: 6.34 us -> 0 us
  Pallas kernels: 130 us -> 128 us
    unnamed x3 -> x0, local copies, waits for them, and re-layouts: 6.34 us -> none
    pallas_call x1 -> x2, Pallas kernels: 130 us -> 128 us  [the longest x1 125 us: on_device(): pl.pallas_call(kernel, out_shape=(jax.ShapeDtypeStruct((8, 16, HALF), BF1...]
where the time goes in v2:
time: 129 us
  Pallas kernels  128 us (99%)
    pallas_call x1, Pallas kernels, on_device(): pl.pallas_call(kernel, out_shape=(jax.ShapeDtypeStruct((8, 16, HALF), BF1...  125 us
    pallas_call x1, Pallas kernels, on_device(): pl.pallas_call(finish, out_shape=(jax.ShapeDtypeStruct((1, 8, WIDTH), BF1...  2.92 us

profile of v2, /device:TPU:1, one launch (start us, length us, event | category | flops | bytes accessed | tf_op | source)
XLA Modules:
  0.0 128.6 jit_solution(9683745477462065360)
XLA Ops:
  0.6 125.1 %gated_backward.1 = (bf16[8,16,1024]{2,1,0:T(8,128)(2,1)}, bf16[8,16,32,128]{3,2,1,0:T(8,128)(2,1)}, f32[2,16,1664]{2,1,0:T(8,128)}) custom-call(bf16[1,8,16384]{2,1,0:T(8,128)(2,1)} %x_hbm.1, bf16[1,8,16384]{2,1,0:T(8,128)(2,1)} %dy_hbm.1, bf16[1,128,1664]{2,1,0:T(8,128)(2,1)} %g_hbm.1, bf16[1,128,1664]{2,1,0:T(8,128)(2,1)} %u_hbm.1, ...), custom_call_target="tpu_custom_call" | custom-call | tf_op jit(solution)/shard_map/gated_backward/pallas_call | solution.py:704
  125.7 2.9 %finish.1 = (bf16[1,8,16384]{2,1,0:T(8,128)(2,1)}, f32[32,16384]{1,0:T(8,128)}, f32[2,16,1664]{2,1,0:T(8,128)}) custom-call(bf16[8,16,1024]{2,1,0:T(8,128)(2,1)} %get-tuple-element.9.v_ref, bf16[8,16,32,128]{3,2,1,0:T(8,128)(2,1)} %get-tuple-element.10.e_ref, f32[2,16,1664]{2,1,0:T(8,128)} %get-tuple-element.11.up_in), custom_call_target="tpu_custom_call" | custom-call | tf_op jit(solution)/shard_map/finish/pallas_call | solution.py:726

commit v3 on v2

--- a/solution.py
+++ b/solution.py
@@ -139,12 +139,12 @@
             )[0]
         r_buf[slot, d] = s_buf[slot, d]
 
-    loaded("g", "u")
-    lax.fori_loop(0, 8, factors, 0)
     loaded("h", "dy")
     rotate(dy_ref, 0)
     pl.semaphore_wait(barrier, 22)
     exchange(0)
+    loaded("g", "u")
+    lax.fori_loop(0, 8, factors, 0)
 
     class ZGather:
         def __init__(self, whole, half):
@@ -192,9 +192,6 @@
         lambda u, core, i: ab.at[u, i, core],
     )
     ab_gather.begin()
-    loaded("x")
-    rotate(x_ref, 1)
-    exchange(1)
 
     def unpack(slot, u):
         low = r_buf[slot, 2 * u].astype(F32)
@@ -290,6 +287,9 @@
     loads["wd"].start()
     ag_step1(0)
     ag_step0(1)
+    loaded("x")
+    rotate(x_ref, 1)
+    exchange(1)
     ag_step2(0)
     ag_step3(0)
     ag_step1(1)
@@ -400,9 +400,6 @@
     k_g1 = send(p_buf.at[2, c], gz_buf.at[1], down_dev)[0]
     ag_step5(2)
     product1(3)
-    adapters_on()
-    inputs_in()
-    loaded("wg", "wu")
     arrived(core_keys[3], q_buf.at[3])
     add_rows((own[3], own[3]), [(q_buf.at[3], 0)])
     ab_gather.across()
@@ -418,6 +415,8 @@
         None,
     )
     d_gather.begin()
+    adapters_on()
+    loaded("wg", "wu")
 
     rs_keys = {}
 
@@ -450,18 +449,18 @@
         zs[:, u, :, : 2 * RANK] = by_token(ranks).astype(BF16).reshape(16, 16, 2 * RANK)
         return (SCALE * ranks).astype(BF16)
 
-    def product2(rel, ranks, h):
+    def second(rel, ranks):
         u = unit(rel)
 
         def body(n, carry):
-            rows = pl.ds(pl.multiple_of(HALF * h + n * TILE2, TILE2), TILE2)
+            rows = pl.ds(pl.multiple_of(n * TILE2, TILE2), TILE2)
             value = lax.dot_general(ab[u, 0].reshape(256, HID), wg[rows, :], NT, preferred_element_type=F32)
             value = value + lax.dot_general(ab[u, 1].reshape(256, HID), wu[rows, :], NT, preferred_element_type=F32)
             value = value + jnp.dot(ranks, a_own[:, rows], preferred_element_type=F32)
             o_buf[u, :, :, :, rows] = by_token(value).astype(BF16).reshape(4, 4, 16, TILE2)
             return carry
 
-        lax.fori_loop(0, HALF // TILE2, body, 0)
+        lax.fori_loop(0, SLICE // TILE2, body, 0)
 
     RAXES = (("y", "x"), ("x", "y"))
 
@@ -548,12 +547,11 @@
 
     steps = (rs_step1, rs_step2, rs_step3, rs_step4, rs_step5)
 
-    items = [(rel, h) for rel in ORDER2 for h in (0, 1)]
-
     def advance(turn):
         for k in range(5):
-            if 0 <= turn - k < 8:
-                steps[k](*items[turn - k])
+            if 0 <= turn - k < 4:
+                for h in (0, 1):
+                    steps[k](ORDER2[turn - k], h)
 
     def z_sum():
         for i in range(1, 16):
@@ -599,11 +597,9 @@
 
     d_gather.have(0)
     gradients(0)
-    ranks = rank_terms(0)
-    product2(0, ranks, 0)
+    second(0, rank_terms(0))
     advance(0)
-    product2(0, ranks, 1)
-    advance(1)
+    inputs_in()
     d_gather.across()
     d_gather.have(3)
     gradients(3)
@@ -611,48 +607,38 @@
     d_gather.have(1)
     gradients(1)
     ab_gather.pass_down()
-    ranks = rank_terms(3)
-    product2(3, ranks, 0)
+    second(3, rank_terms(3))
+    advance(1)
+    second(1, rank_terms(1))
+    ab_gather.last()
     advance(2)
-    product2(3, ranks, 1)
-    advance(3)
-    ranks = rank_terms(1)
-    product2(1, ranks, 0)
-    advance(4)
-    product2(1, ranks, 1)
-    ab_gather.last()
-    advance(5)
     ab_gather.have(2)
     ranks = rank_terms(2)
     for i in range(1, 16):
         to = (t + i) % 16
         z_keys[i] = send(zs.at[to], zr.at[t], (d, to))[0]
-    product2(2, ranks, 0)
-    advance(6)
+    second(2, ranks)
+    advance(3)
     z_sum()
-    product2(2, ranks, 1)
-    advance(7)
+    advance(4)
     down_sum()
-    for i in range(1, 16):
-        arrived(adt_keys[i], adn.at[(t + 16 - i) % 16])
-    up_grads(0)
-    up_grads(3)
-    advance(8)
+    advance(5)
     for i in range(1, 16):
         arrived(piece_keys[i], e_buf.at[d, (t + 16 - i) % 16])
     e_gather.begin()
-    advance(9)
-    up_grads(1)
-    up_grads(2)
+    advance(6)
+    for i in range(1, 16):
+        arrived(adt_keys[i], adn.at[(t + 16 - i) % 16])
+    for rel in range(4):
+        up_grads(rel)
     up_ref[0] = grads_up[0][:RANK] * GRAD_SCALE
     up_ref[1] = grads_up[1][RANK:] * GRAD_SCALE
     stores = [pltpu.make_async_copy(up_ref, up_hbm, ws.at[0])]
     stores[0].start()
-    advance(10)
     e_gather.across()
     e_gather.pass_up()
     e_gather.pass_down()
-    advance(11)
+    advance(7)
     e_gather.last()
     for rel in range(4):
         e_gather.have(rel)

time: 129 us -> 128 us (level)
  no operation moved by 1% of the time
where the time goes in v3:
time: 128 us
  Pallas kernels  128 us (100%)
    pallas_call x1, Pallas kernels, on_device(): pl.pallas_call(kernel, out_shape=(jax.ShapeDtypeStruct((8, 16, HALF), BF1...  125 us
    pallas_call x1, Pallas kernels, on_device(): pl.pallas_call(finish, out_shape=(jax.ShapeDtypeStruct((1, 8, WIDTH), BF1...  2.92 us

profile of v3, /device:TPU:1, one launch (start us, length us, event | category | flops | bytes accessed | tf_op | source)
XLA Modules:
  0.0 128.2 jit_solution(713175643402611282)
XLA Ops:
  0.6 124.6 %gated_backward.1 = (bf16[8,16,1024]{2,1,0:T(8,128)(2,1)}, bf16[8,16,32,128]{3,2,1,0:T(8,128)(2,1)}, f32[2,16,1664]{2,1,0:T(8,128)}) custom-call(bf16[1,8,16384]{2,1,0:T(8,128)(2,1)} %x_hbm.1, bf16[1,8,16384]{2,1,0:T(8,128)(2,1)} %dy_hbm.1, bf16[1,128,1664]{2,1,0:T(8,128)(2,1)} %g_hbm.1, bf16[1,128,1664]{2,1,0:T(8,128)(2,1)} %u_hbm.1, ...), custom_call_target="tpu_custom_call" | custom-call | tf_op jit(solution)/shard_map/gated_backward/pallas_call | solution.py:690
  125.2 2.9 %finish.1 = (bf16[1,8,16384]{2,1,0:T(8,128)(2,1)}, f32[32,16384]{1,0:T(8,128)}, f32[2,16,1664]{2,1,0:T(8,128)}) custom-call(bf16[8,16,1024]{2,1,0:T(8,128)(2,1)} %get-tuple-element.9.v_ref, bf16[8,16,32,128]{3,2,1,0:T(8,128)(2,1)} %get-tuple-element.10.e_ref, f32[2,16,1664]{2,1,0:T(8,128)} %get-tuple-element.11.up_in), custom_call_target="tpu_custom_call" | custom-call | tf_op jit(solution)/shard_map/finish/pallas_call | solution.py:712
